TPU v7x, 32 devices: a whole 2x2x4 slice. The times are simulated.
32 devices in a mesh: section: 2 (over x), win: 4 (over y, core), dp: 4 (over z).
Axes of the slice: x: 2, y: 2, z: 4, core: 2. Of those that a mesh axis runs over, the one named last changes fastest.
Arguments:
- tokens: bfloat16 [2, 4, 4, 64, 1536], P(None, 'win', 'dp'), may hold values from -6 to 6
- regions: int32 [2, 4, 256], P('section', 'win'), may hold values from 0 to 3
- norm_gain: float32 [2, 1536], P('section'), may hold values from 0.1 to 1.9
- qkv_weight: bfloat16 [2, 1536, 3, 1024], P('section', None, None, 'dp'), as said below
- out_weight: bfloat16 [2, 1024, 1536], P('section', 'dp'), may hold values from -2 to 2
- final_gain: float32 [1536], replicated, may hold values from 0.1 to 1.9
- dec_weight: bfloat16 [1536, 1104], P(None, 'section'), may hold values from -0.15625 to 0.15625
Outputs:
- decoded: bfloat16 [2, 4, 4, 64, 1104], P(None, 'win', 'dp', None, 'section')
Inputs may be any that keep to these rules, and one draw needn't show every extreme that they name: `qkv_weight`: entries lie below 80 / sqrt(1536) in magnitude.
All inputs are finite; a program needn't handle non-finite values.
Results may differ from a plain program's by a relative error of at most 0.03.
Values may be sent and summed in bfloat16 or wider, within the bound.
A program may use at most 64 MiB of HBM per device.

v0:
```python
import math

import jax
import jax.numpy as jnp
from jax import lax
from jax.sharding import PartitionSpec as P

HEAD_DIM = 64


def from_behind(value, axis, steps):
    count = lax.axis_size(axis)
    pairs = [(source, (source + steps) % count) for source in range(count)]
    return lax.ppermute(value, axis, pairs)


def shifted(value, axis, steps):
    count = lax.axis_size(axis)
    leading, last = (max(0, -steps), min(count, count - steps))
    return lax.ppermute(value, axis, [(source, source + steps) for source in range(leading, last)])


def from_root(block, axis, holder):
    block = jnp.where(lax.axis_index(axis) == holder, block, jnp.zeros_like(block))
    return lax.psum(block, axis)


def normalize(hidden, scales):
    values = hidden.astype(jnp.float32)
    center = values - jnp.mean(values, axis=-1, keepdims=True)
    spread = jnp.mean(center * center, axis=-1, keepdims=True)
    return (center * lax.rsqrt(spread + 1e-05) * scales).astype(jnp.bfloat16)


def rounded(values):
    return lax.optimization_barrier(values.astype(jnp.bfloat16)).astype(jnp.float32)


def attend(projected, labels, head_size):
    row_count = projected.shape[0]
    inner_width = projected.shape[2]
    head_count = inner_width // head_size
    queries = projected[:, 0].reshape(row_count, head_count, head_size)
    keys_all = projected[:, 1].reshape(row_count, head_count, head_size)
    values_all = projected[:, 2].reshape(row_count, head_count, head_size)
    scores = jnp.einsum(
        "qhe,khe->hqk", queries, keys_all, preferred_element_type=jnp.float32
    ) / math.sqrt(head_size)
    allowed = labels[:, None] == labels[None, :]
    scores = jnp.where(allowed[None], scores, -jnp.inf)
    largest = jnp.max(scores, axis=-1, keepdims=True)
    weights = jnp.exp(scores - largest)
    shares = (weights / jnp.sum(weights, axis=-1, keepdims=True)).astype(jnp.bfloat16)
    blended = jnp.einsum("hqk,khe->qhe", shares, values_all, preferred_element_type=jnp.float32)
    return blended.astype(jnp.bfloat16).reshape(row_count, inner_width)


def body(tokens, regions, norm_gain, qkv_weight, out_weight, final_gain, dec_weight):
    sections = lax.axis_size("section")
    section_index = lax.axis_index("section")
    micro_count = tokens.shape[0]
    quad_rows = tokens.shape[3]
    half_rows = quad_rows // 2
    labels = regions[0, 0]
    layer_gain = norm_gain[0]
    projection = qkv_weight[0]
    out_local = out_weight[0]
    empty = jnp.zeros(tokens.shape[3:], jnp.bfloat16)
    incoming = empty
    finished = []
    for moment in range(micro_count + sections - 1):
        fresh = tokens[moment, 0, 0] if moment < micro_count else empty
        current = jnp.where(section_index == 0, fresh, incoming)
        normed = normalize(current, layer_gain)
        projected = jnp.einsum(
            "td,dcf->tcf",
            lax.all_gather(normed, "dp", axis=0, tiled=True),
            projection,
            preferred_element_type=jnp.float32,
        ).astype(jnp.bfloat16)
        blended = attend(projected, labels, HEAD_DIM)
        update = lax.psum_scatter(
            rounded(jnp.dot(blended, out_local, preferred_element_type=jnp.float32)).astype(
                jnp.bfloat16
            ),
            "dp",
            scatter_dimension=0,
            tiled=True,
        ).astype(jnp.float32)
        hidden = (current.astype(jnp.float32) + update).astype(jnp.bfloat16)
        arriving = from_behind(hidden[:half_rows], "win", -1)
        result = jnp.concatenate([hidden[half_rows:], arriving], axis=0)
        if moment >= sections - 1:
            finished.append(result)
        if moment < micro_count + sections - 2:
            incoming = shifted(result, "section", 1)
    collected = jnp.stack(finished)
    final = normalize(collected, final_gain)
    shared = from_root(final, "section", sections - 1)
    decoded = jnp.einsum(
        "mtd,dc->mtc", shared, dec_weight, preferred_element_type=jnp.float32
    ).astype(jnp.bfloat16)
    return decoded[:, None, None]


def solution(mesh):
    return jax.shard_map(
        body,
        mesh=mesh,
        in_specs=(
            P(None, "win", "dp", None, None),
            P("section", "win", None),
            P("section", None),
            P("section", None, None, "dp"),
            P("section", "dp", None),
            P(),
            P(None, "section"),
        ),
        out_specs=P(None, "win", "dp", None, "section"),
        check_vma=False,
    )
```

profile of v0, /device:TPU:0, one launch (start us, length us, event | category | flops | bytes accessed | tf_op | source)
XLA Modules:
  0.0 232.5 jit_solution(2507135951319407794)
XLA Ops:
  11.6 21.3 %all_gather.9 = bf16[256,1536]{1,0:T(8,128)(2,1)S(1)} all-gather(bf16[64,1536]{1,0:T(8,128)(2,1)S(1)} %fusion.62), channel_id=1, replica_groups=mesh['section'=2,'win'=4,'dp'=4] {'dp'}, dimensions={0}, use_global_device_ids=true | all-gather | bytes 983040 | tf_op jit(solution)/shard_map/all_gather | solution.py:77
  35.9 2.7 %convolution_convert_fusion.5 = bf16[4,64,256]{2,1,0:T(8,128)(2,1)} fusion(bf16[256,4,64]{0,2,1:T(8,128)(2,1)S(1)} %bitcast.119, f32[4,256]{1,0:T(4,128)S(1)} %fusion.83, f32[4,256,256]{1,2,0:T(8,128)} %fusion.19), kind=kOutput, calls=%fused_computation.32 | convolution fusion | flops 34407680 | bytes 1314816 | tf_op jit(solution)/shard_map/hqk,khe->qhe/dot_general | solution.py:54
  38.5 2.2 convolution_convert_fusion.2
  40.8 22.8 %reduce-scatter.4.cloned.1.call-done = bf16[64,1536]{1,0:T(8,128)(2,1)} async-done(((bf16[256,1536]{1,0:T(8,128)(2,1)}), bf16[64,1536]{1,0:T(8,128)(2,1)}) %reduce-scatter.4.cloned.1.call-update) | async-done | bytes 196624 | tf_op jit(solution)/shard_map/reduce_scatter | solution.py:82
  64.7 2.2 collective-permute-done
  66.9 3.3 %collective-permute-start.1 = (bf16[64,1536]{1,0:T(8,128)(2,1)S(1)}, bf16[64,1536]{1,0:T(8,128)(2,1)S(1)}, u32[]{:S(2)}, u32[]{:S(2)}) collective-permute-start(bf16[64,1536]{1,0:T(8,128)(2,1)S(1)} %pad_maximum_fusion.1), channel_id=1, source_target_pairs={{0,16},{1,17},{2,18},{3,19},{4,20},{5,21},{6,22},{7,23},{8,24},{9,... | collective-permute-start | bytes 589832 | tf_op jit(solution)/shard_map/ppermute | solution.py:20
  70.3 4.6 %collective-permute-done.1 = bf16[64,1536]{1,0:T(8,128)(2,1)S(1)} collective-permute-done((bf16[64,1536]{1,0:T(8,128)(2,1)S(1)}, bf16[64,1536]{1,0:T(8,128)(2,1)S(1)}, u32[]{:S(2)}, u32[]{:S(2)}) %collective-permute-start.1) | collective-permute-done | bytes 196640 | tf_op jit(solution)/shard_map/ppermute | solution.py:20
  76.4 19.0 %all_gather.10 = bf16[256,1536]{1,0:T(8,128)(2,1)S(1)} all-gather(bf16[64,1536]{1,0:T(8,128)(2,1)S(1)} %fusion.59), channel_id=1, replica_groups=mesh['section'=2,'win'=4,'dp'=4] {'dp'}, dimensions={0}, use_global_device_ids=true | all-gather | bytes 983040 | tf_op jit(solution)/shard_map/all_gather | solution.py:77
  97.1 1.4 fusion.84
  98.6 2.2 fusion.18
  100.8 2.0 convolution_convert_fusion.4
  104.1 23.3 %reduce-scatter.6.cloned.1.call-done = bf16[64,1536]{1,0:T(8,128)(2,1)} async-done(((bf16[256,1536]{1,0:T(8,128)(2,1)}), bf16[64,1536]{1,0:T(8,128)(2,1)}) %reduce-scatter.6.cloned.1.call-update) | async-done | bytes 196624 | tf_op jit(solution)/shard_map/reduce_scatter | solution.py:82
  128.5 2.2 collective-permute-done.2
  130.8 3.3 %collective-permute-start.3 = (bf16[64,1536]{1,0:T(8,128)(2,1)S(1)}, bf16[64,1536]{1,0:T(8,128)(2,1)S(1)}, u32[]{:S(2)}, u32[]{:S(2)}) collective-permute-start(bf16[64,1536]{1,0:T(8,128)(2,1)S(1)} %get-tuple-element.17), channel_id=1, source_target_pairs={{0,16},{1,17},{2,18},{3,19},{4,20},{5,21},{6,22},{7,23},{8,24},{9,... | collective-permute-start | bytes 589832 | tf_op jit(solution)/shard_map/ppermute | solution.py:20
  134.1 4.5 %collective-permute-done.3 = bf16[64,1536]{1,0:T(8,128)(2,1)S(1)} collective-permute-done((bf16[64,1536]{1,0:T(8,128)(2,1)S(1)}, bf16[64,1536]{1,0:T(8,128)(2,1)S(1)}, u32[]{:S(2)}, u32[]{:S(2)}) %collective-permute-start.3) | collective-permute-done | bytes 196640 | tf_op jit(solution)/shard_map/ppermute | solution.py:20
  139.1 19.1 %all_gather.11 = bf16[256,1536]{1,0:T(8,128)(2,1)S(1)} all-gather(bf16[64,1536]{1,0:T(8,128)(2,1)S(1)} %fusion.56), channel_id=1, replica_groups=mesh['section'=2,'win'=4,'dp'=4] {'dp'}, dimensions={0}, use_global_device_ids=true | all-gather | bytes 983040 | tf_op jit(solution)/shard_map/all_gather | solution.py:77
  160.0 1.5 fusion.85
  161.5 2.3 fusion.17
  163.8 2.6 %convolution_convert_fusion.3 = bf16[4,64,256]{2,1,0:T(8,128)(2,1)} fusion(bf16[256,4,64]{0,2,1:T(8,128)(2,1)} %bitcast.118, f32[4,256]{1,0:T(4,128)S(1)} %fusion.85, f32[4,256,256]{1,2,0:T(8,128)} %fusion.17), kind=kOutput, calls=%fused_computation.30 | convolution fusion | flops 34407680 | bytes 1314816 | tf_op jit(solution)/shard_map/hqk,khe->qhe/dot_general | solution.py:54
  166.5 2.2 convolution_convert_fusion
  168.7 23.2 %reduce-scatter.8.cloned.1.call-done = bf16[64,1536]{1,0:T(8,128)(2,1)} async-done(((bf16[256,1536]{1,0:T(8,128)(2,1)}), bf16[64,1536]{1,0:T(8,128)(2,1)}) %reduce-scatter.8.cloned.1.call-update) | async-done | bytes 196624 | tf_op jit(solution)/shard_map/reduce_scatter | solution.py:82
  193.0 2.2 collective-permute-done.4
  196.8 26.2 %all-reduce.2.cloned.1.call-done = bf16[2,64,1536]{2,1,0:T(8,128)(2,1)} async-done(((bf16[2,64,1536]{2,1,0:T(8,128)(2,1)}), bf16[2,64,1536]{2,1,0:T(8,128)(2,1)}) %all-reduce.2.cloned.1.call-update) | async-done | bytes 393232 | tf_op jit(solution)/shard_map/psum | solution.py:25
  222.9 3.0 %fusion.32 = bf16[2,1,1,64,552]{4,3,2,1,0:T(8,128)(2,1)} fusion(bf16[2,64,1536]{2,1,0:T(8,128)(2,1)} %all-reduce.2.cloned.1.call-done, bf16[1536,552]{0,1:T(8,128)(2,1)} %param.13), kind=kOutput, calls=%fused_computation.33 | convolution fusion | flops 217125888 | bytes 2230272 | tf_op jit(solution)/shard_map/mtd,dc->mtc/dot_general | solution.py:100
  (63 shorter events, 19.6 us)
Async XLA Ops:
  6.5 26.4 %copy-start = (bf16[1,1536,3,256]{3,1,2,0:T(8,128)(2,1)S(1)}, bf16[1,1536,3,256]{3,1,2,0:T(8,128)(2,1)}, u32[]{:S(2)}) copy-start(bf16[1,1536,3,256]{3,1,2,0:T(8,128)(2,1)} %param.10) | copy-start | bytes 7077892
  6.5 57.1 %reduce-scatter.4.cloned.1.call-start = ((), (), s32[]{:S(2)}) async-start(), calls=%async_computation.3 | async-start | bytes 983040 | tf_op jit(solution)/shard_map/reduce_scatter | solution.py:82
  9.8 24.7 %copy-start.3 = (pred[256,256]{0,1:T(8,128)(4,1)}, pred[256,256]{0,1:T(8,128)(4,1)S(1)}, u32[]{:S(2)}) copy-start(pred[256,256]{0,1:T(8,128)(4,1)S(1)} %broadcast_compare_fusion) | copy-start | bytes 196612
  35.9 2.7 %copy-start.1 = (bf16[1,256,1536]{2,1,0:T(8,128)(2,1)S(1)}, bf16[1,256,1536]{2,1,0:T(8,128)(2,1)}, u32[]{:S(2)}) copy-start(bf16[1,256,1536]{2,1,0:T(8,128)(2,1)} %param.11) | copy-start | bytes 2359300
  38.5 25.1 %copy-start.2 = (bf16[2,1,1,64,1536]{4,3,2,1,0:T(8,128)(2,1)S(1)}, bf16[2,1,1,64,1536]{4,3,2,1,0:T(8,128)(2,1)}, u32[]{:S(2)}) copy-start(bf16[2,1,1,64,1536]{4,3,2,1,0:T(8,128)(2,1)} %param.7) | copy-start | bytes 1179652
  40.8 86.7 %reduce-scatter.6.cloned.1.call-start = ((), (), s32[]{:S(2)}) async-start(), calls=%async_computation.4 | async-start | bytes 983040 | tf_op jit(solution)/shard_map/reduce_scatter | solution.py:82
  64.6 2.3 collective-permute-start
  66.9 7.9 %collective-permute-start.1 = (bf16[64,1536]{1,0:T(8,128)(2,1)S(1)}, bf16[64,1536]{1,0:T(8,128)(2,1)S(1)}, u32[]{:S(2)}, u32[]{:S(2)}) collective-permute-start(bf16[64,1536]{1,0:T(8,128)(2,1)S(1)} %pad_maximum_fusion.1), channel_id=1, source_target_pairs={{0,16},{1,17},{2,18},{3,19},{4,20},{5,21},{6,22},{7,23},{8,24},{9,... | collective-permute-start | bytes 589832 | tf_op jit(solution)/shard_map/ppermute | solution.py:20
  95.4 1.8 copy-start.4
  104.1 87.9 %reduce-scatter.8.cloned.1.call-start = ((), (), s32[]{:S(2)}) async-start(), calls=%async_computation.5 | async-start | bytes 983040 | tf_op jit(solution)/shard_map/reduce_scatter | solution.py:82
  128.5 2.3 collective-permute-start.2
  130.8 7.9 %collective-permute-start.3 = (bf16[64,1536]{1,0:T(8,128)(2,1)S(1)}, bf16[64,1536]{1,0:T(8,128)(2,1)S(1)}, u32[]{:S(2)}, u32[]{:S(2)}) collective-permute-start(bf16[64,1536]{1,0:T(8,128)(2,1)S(1)} %get-tuple-element.17), channel_id=1, source_target_pairs={{0,16},{1,17},{2,18},{3,19},{4,20},{5,21},{6,22},{7,23},{8,24},{9,... | collective-permute-start | bytes 589832 | tf_op jit(solution)/shard_map/ppermute | solution.py:20
  166.5 29.2 %copy-start.5 = (f32[1536]{0:T(1024)S(1)}, f32[1536]{0:T(1024)}, u32[]{:S(2)}) copy-start(f32[1536]{0:T(1024)} %param.12) | copy-start | bytes 18436
  168.7 54.3 %all-reduce.2.cloned.1.call-start = ((), (), s32[]{:S(2)}) async-start(), calls=%async_computation.6 | async-start | bytes 786432 | tf_op jit(solution)/shard_map/psum | solution.py:25
  193.0 2.3 collective-permute-start.4
Sparse Core Ops, SparseCore 0:
  40.9 22.6 reduce-scatter.3
  104.2 23.2 reduce-scatter.5
  168.8 23.1 reduce-scatter.7
  196.9 26.0 all-reduce.1
where the time goes:
time: 233 us; the launch traced here: 232 us
  waiting for transfers between devices  111 us (48%)
  blocking collectives  59.4 us (25%)
  matrix products  28.4 us (12%)
  between operations  13.3 us (6%)
  other arithmetic  11.5 us (5%)
  starting transfers between devices  6.95 us (3%)
    reduce_scatter x3, waiting for transfers between devices, body(): lax.psum_scatter(rounded(jnp.dot(blended, out_local, preferred_element_ty...  69.4 us
    all_gather x3, blocking collectives, body(): lax.all_gather(normed, 'dp', axis=0, tiled=True)  59.4 us
    psum x1, waiting for transfers between devices, from_root(): return lax.psum(block, axis)  26.2 us
    ppermute x2, waiting for transfers between devices, shifted(): lax.ppermute(value, axis, [(source, source + steps) for source in range(l...  9.12 us
    dot_general x3, matrix products, attend(): jnp.einsum('hqk,khe->qhe', shares, values_all, preferred_element_type=jnp...  7.25 us
    ppermute x2, starting transfers between devices, shifted(): lax.ppermute(value, axis, [(source, source + steps) for source in range(l...  6.66 us
    ppermute x3, waiting for transfers between devices, from_behind(): return lax.ppermute(value, axis, pairs)  6.62 us
    dot_general x3, matrix products, attend(): jnp.einsum('qhe,khe->hqk', queries, keys_all, preferred_element_type=jnp....  5.88 us
  transfers between devices with their start and end apart: 9, of which 9 were waited for; matrix products, arithmetic and copies ran while one was open for 0% of the time, Pallas kernels for 0%

commit v1 on v0

v1 whole, which is shorter than its diff:
```python
import functools
import math

import jax
import jax.numpy as jnp
from jax import lax
from jax.experimental import pallas as pl
from jax.experimental.pallas import tpu as pltpu
from jax.sharding import PartitionSpec as P

HEAD_DIM = 64
MESH = pl.DeviceIdType.MESH
EXCLUDED = -1e30


def normalize(hidden, scales):
    values = hidden.astype(jnp.float32)
    center = values - jnp.mean(values, axis=-1, keepdims=True)
    spread = jnp.mean(center * center, axis=-1, keepdims=True)
    return (center * lax.rsqrt(spread + 1e-05) * scales).astype(jnp.bfloat16)


def kernel(
    sections, windows, bands,
    tokens, labels, gain, wqkv_hbm, wout_hbm, final_gain, wdec_hbm,
    decoded,
    full, relay, normed, projected, wqkv, wout, wdec, bias, bstage, blend, hstage, fstage, final,
    ag_send, ag_recv, a2a_send, a2a_recv, hid_send, hid_recv, fin_send, fin_recv,
    rel_send, rel_recv, fwd_send, wz_send, wz_recv, wy_send, wy_recv, wc_send, wc_recv, load_sem,
):
    micros, quad, width = tokens.shape
    half = quad // 2
    last = sections - 1
    s = lax.axis_index("section")
    w = lax.axis_index("win")
    b = lax.axis_index("dp")
    before = lax.rem(w + windows - 1, windows)
    after = lax.rem(w + 1, windows)
    core_peer = w + 1 - 2 * lax.rem(w, 2)
    chip_peer = w + 2 - 4 * lax.rem(w // 2, 2)
    quarter = lax.rem(w, 4)
    group_rows = wout_hbm.shape[0]
    piece = group_rows // 4

    def band(k):
        return lax.rem(b + k, bands)

    def send(src, dst, send_sem, recv_sem, device):
        return pltpu.make_async_remote_copy(
            src_ref=src, dst_ref=dst, send_sem=send_sem, recv_sem=recv_sem,
            device_id=device, device_id_type=MESH,
        )

    def ag_copy(m, k):
        return send(full.at[m, b], full.at[m, b], ag_send.at[m, k - 1],
                    ag_recv.at[m, bands - k - 1], (s, w, band(k)))

    def ag_arrival(m, k):
        slot = full.at[m, band(k)]
        return send(slot, slot, ag_send.at[m, k - 1], ag_recv.at[m, k - 1], (s, w, band(k)))

    def relay_copy(k):
        return send(relay.at[b], relay.at[b], rel_send.at[k - 1],
                    rel_recv.at[bands - k - 1], (s, w, band(k)))

    def relay_arrival(k):
        slot = relay.at[band(k)]
        return send(slot, slot, rel_send.at[k - 1], rel_recv.at[k - 1], (s, w, band(k)))

    def forward_copy(k):
        return send(relay.at[band(k)], full.at[1, band(k)], fwd_send.at[k - 1],
                    ag_recv.at[1, k - 1], (0, w, b))

    def a2a_copy(m, k):
        return send(bstage.at[m, band(k)], blend.at[m, b], a2a_send.at[m, k - 1],
                    a2a_recv.at[m, bands - k - 1], (s, w, band(k)))

    def a2a_arrival(m, k):
        slot = blend.at[m, band(k)]
        return send(slot, slot, a2a_send.at[m, k - 1], a2a_recv.at[m, k - 1], (s, w, band(k)))

    def wz_copy(k):
        rows = pl.ds(pl.multiple_of(quarter * piece, piece), piece)
        return send(wout_hbm.at[rows], wout.at[b, rows], wz_send.at[k - 1],
                    wz_recv.at[bands - k - 1], (s, w, band(k)))

    def w_piece(k, owner):
        return wout.at[band(k), pl.ds(pl.multiple_of(lax.rem(owner, 4) * piece, piece), piece)]

    def wz_arrival(k):
        slot = w_piece(k, w)
        return send(slot, slot, wz_send.at[k - 1], wz_recv.at[k - 1], (s, w, band(k)))

    def wy_copy(k):
        slot = w_piece(k, w)
        return send(slot, slot, wy_send.at[k - 1], wy_recv.at[k - 1], (s, chip_peer, b))

    def wy_arrival(k):
        slot = w_piece(k, chip_peer)
        return send(slot, slot, wy_send.at[k - 1], wy_recv.at[k - 1], (s, chip_peer, b))

    def wc_copy(k, far):
        slot = w_piece(k, chip_peer if far else w)
        index = 3 * far + k - 1
        return send(slot, slot, wc_send.at[index], wc_recv.at[index], (s, core_peer, b))

    def wc_arrival(k, far):
        other = core_peer + 2 - 4 * lax.rem(core_peer // 2, 2)
        slot = w_piece(k, other if far else core_peer)
        index = 3 * far + k - 1
        return send(slot, slot, wc_send.at[index], wc_recv.at[index], (s, core_peer, b))

    def hidden_copy(m, part):
        rows_from = pl.ds(half * (1 - part), half)
        rows_to = pl.ds(half * part, half)
        return send(hstage.at[m, rows_from], full.at[m, b, rows_to], hid_send.at[m, part],
                    hid_recv.at[m, part], (s + 1, before if part else w, b))

    def hidden_arrival(m, part):
        slot = full.at[m, b, pl.ds(half * part, half)]
        return send(slot, slot, hid_send.at[m, part], hid_recv.at[m, part], (s, after, b))

    def final_copy(m, to, part):
        rows_from = pl.ds(half * (1 - part), half)
        rows_to = pl.ds(half * part, half)
        return send(fstage.at[m, rows_from], final.at[m, rows_to], fin_send.at[m, to, part],
                    fin_recv.at[m, part], (to, before if part else w, b))

    def final_arrival(m, part):
        slot = final.at[m, pl.ds(half * part, half)]
        return send(slot, slot, fin_send.at[m, 0, part], fin_recv.at[m, part], (s, after, b))

    others = range(1, bands)

    load_qkv = pltpu.make_async_copy(wqkv_hbm, wqkv, load_sem.at[0])
    load_out = pltpu.make_async_copy(wout_hbm, wout.at[b], load_sem.at[1])
    load_dec = pltpu.make_async_copy(wdec_hbm, wdec, load_sem.at[2])
    load_qkv.start()
    load_out.start()
    load_dec.start()

    barrier = pltpu.get_barrier_semaphore()
    partners = [(s, w, band(k)) for k in others]
    partners += [(s, core_peer, b), (s, chip_peer, b)]
    partners += [(lax.rem(s + k, sections), w, b) for k in range(1, sections)]
    for to in range(sections):
        partners += [(to, before, b), (to, after, b)]
    for device in partners:
        pl.semaphore_signal(barrier, inc=1, device_id=device, device_id_type=MESH)

    @pl.when(s == 0)
    def _():
        for m in range(micros):
            full[m, b] = tokens[m]

    @pl.when(s == 1)
    def _():
        relay[b] = tokens[1]

    pl.semaphore_wait(barrier, len(partners))

    def start_gather(m):
        @pl.when(s > 0)
        def _():
            for part in range(2):
                hidden_arrival(m, part).wait_recv()

        if m == 1:
            @pl.when(s > 0)
            def _():
                for k in others:
                    ag_copy(m, k).start()
        else:
            for k in others:
                ag_copy(m, k).start()

    def start_weights():
        for k in others:
            wz_copy(k).start()

    def weights_over_chips():
        for k in others:
            wz_arrival(k).wait_recv()
            wy_copy(k).start()
            wc_copy(k, 0).start()

    def weights_over_cores():
        for k in others:
            wy_arrival(k).wait_recv()
            wc_copy(k, 1).start()

    def weights_all():
        for k in others:
            wc_arrival(k, 0).wait_recv()
            wc_arrival(k, 1).wait_recv()

    def normalize_band(m, slot):
        rows = pl.ds(pl.multiple_of(slot * quad, quad), quad)
        normed[rows, :] = normalize(full[m, slot], gain[...])

    def project(m):
        normalize_band(m, b)
        for k in others:
            ag_arrival(m, k).wait_recv()
            normalize_band(m, band(k))
        if m == 0:
            load_qkv.wait()
        for c in range(3):
            projected[c] = jnp.dot(
                normed[...], wqkv[c], preferred_element_type=jnp.float32
            ).astype(jnp.bfloat16)

    def attend(m):
        inner = projected.shape[2]
        rows = projected.shape[1]
        lane = lax.broadcasted_iota(jnp.int32, (rows, 128), 1)
        for pair in range(inner // 128):
            columns = slice(128 * pair, 128 * pair + 128)
            queries = projected[0, :, columns]
            keys_all = projected[1, :, columns]
            values_all = projected[2, :, columns]
            results = []
            for side in range(128 // HEAD_DIM):
                mine = (lane // HEAD_DIM) == side
                query = jnp.where(mine, queries, jnp.zeros_like(queries))
                scores = lax.dot_general(
                    query, keys_all, (((1,), (1,)), ((), ())), preferred_element_type=jnp.float32
                ) * (1.0 / math.sqrt(HEAD_DIM)) + bias[...]
                largest = jnp.max(scores, axis=-1, keepdims=True)
                weights = jnp.exp(scores - largest)
                total = jnp.sum(weights, axis=-1, keepdims=True)
                product = jnp.dot(
                    weights.astype(jnp.bfloat16), values_all, preferred_element_type=jnp.float32
                )
                results.append(product / total)
            mixed = results[0]
            for side in range(1, 128 // HEAD_DIM):
                mixed = jnp.where((lane // HEAD_DIM) == side, results[side], mixed)
            mixed = mixed.astype(jnp.bfloat16)
            for place in range(bands):
                bstage[m, place, :, columns] = mixed[place * quad:(place + 1) * quad]
        for k in others:
            a2a_copy(m, k).start()
        blend[m, b] = bstage[m, b]

    def finish(m):
        for k in others:
            a2a_arrival(m, k).wait_recv()
        for start in range(0, width, 512):
            columns = slice(start, start + 512)
            total = full[m, b, :, columns].astype(jnp.float32)
            for group in range(bands):
                total += jnp.dot(
                    blend[m, group], wout[group, :, columns], preferred_element_type=jnp.float32
                )
            hstage[m, :, columns] = total.astype(jnp.bfloat16)

        @pl.when(s < last)
        def _():
            for part in range(2):
                hidden_copy(m, part).start()

        @pl.when(s == last)
        def _():
            fstage[m] = normalize(hstage[m], final_gain[...])
            for to in range(sections):
                final_copy(m, to, 1).start()
                if to != last:
                    final_copy(m, to, 0).start()
            final[m, :half] = fstage[m, half:]

    def decode(m):
        @pl.when(s < last)
        def _():
            final_arrival(m, 0).wait_recv()

        final_arrival(m, 1).wait_recv()
        decoded[m] = lax.dot_general(
            final[m], wdec[...], (((1,), (1,)), ((), ())), preferred_element_type=jnp.float32
        ).astype(jnp.bfloat16)

    @pl.when(s == 1)
    def _():
        for k in others:
            relay_copy(k).start()

    @pl.when(s > 0)
    def _():
        start_weights()

    row = labels[...].astype(jnp.float32)
    across = jnp.broadcast_to(row, bias.shape)
    bias[...] = jnp.where(across == across.T, 0.0, EXCLUDED)

    @pl.when(s == 1)
    def _():
        for k in others:
            relay_arrival(k).wait_recv()
            forward_copy(k).start()

    @pl.when(s > 0)
    def _():
        weights_over_chips()
        weights_over_cores()

    start_gather(0)

    @pl.when(s == 0)
    def _():
        start_weights()

    project(0)
    start_gather(1)

    @pl.when(s == 0)
    def _():
        weights_over_chips()

    attend(0)

    @pl.when(s == 0)
    def _():
        weights_over_cores()

    load_out.wait()
    weights_all()
    finish(0)
    project(1)
    attend(1)
    finish(1)
    load_dec.wait()
    decode(0)
    decode(1)

    for m in range(micros):
        for k in others:
            a2a_copy(m, k).wait_send()
            if m != 1:
                ag_copy(m, k).wait_send()
    for k in others:
        wz_copy(k).wait_send()
        wy_copy(k).wait_send()
        wc_copy(k, 0).wait_send()
        wc_copy(k, 1).wait_send()

    @pl.when(s > 0)
    def _():
        for k in others:
            ag_copy(1, k).wait_send()

    @pl.when(s == 1)
    def _():
        for k in others:
            relay_copy(k).wait_send()
            forward_copy(k).wait_send()

    @pl.when(s < last)
    def _():
        for m in range(micros):
            for part in range(2):
                hidden_copy(m, part).wait_send()

    @pl.when(s == last)
    def _():
        for m in range(micros):
            for to in range(sections):
                final_copy(m, to, 1).wait_send()
                if to != last:
                    final_copy(m, to, 0).wait_send()


def body(sections, windows, bands, tokens, regions, norm_gain, qkv_weight, out_weight, final_gain, dec_weight):
    micros, _, _, quad, width = tokens.shape
    inner = qkv_weight.shape[3]
    columns = dec_weight.shape[1]
    rows = bands * quad
    bf16 = jnp.bfloat16
    vmem = pl.BlockSpec(memory_space=pltpu.VMEM)
    hbm = pl.BlockSpec(memory_space=pl.ANY)
    dma = pltpu.SemaphoreType.DMA
    decoded = pl.pallas_call(
        functools.partial(kernel, sections, windows, bands),
        out_shape=jax.ShapeDtypeStruct((micros, quad, columns), bf16),
        in_specs=[vmem, vmem, vmem, hbm, hbm, vmem, hbm],
        out_specs=vmem,
        scratch_shapes=[
            pltpu.VMEM((micros, bands, quad, width), bf16),
            pltpu.VMEM((bands, quad, width), bf16),
            pltpu.VMEM((rows, width), bf16),
            pltpu.VMEM((3, rows, inner), bf16),
            pltpu.VMEM((3, width, inner), bf16),
            pltpu.VMEM((bands, inner, width), bf16),
            pltpu.VMEM((columns, width), bf16),
            pltpu.VMEM((rows, rows), jnp.float32),
            pltpu.VMEM((micros, bands, quad, inner), bf16),
            pltpu.VMEM((micros, bands, quad, inner), bf16),
            pltpu.VMEM((micros, quad, width), bf16),
            pltpu.VMEM((micros, quad, width), bf16),
            pltpu.VMEM((micros, quad, width), bf16),
            dma((micros, 3)), dma((micros, 3)),
            dma((micros, 3)), dma((micros, 3)),
            dma((micros, 2)), dma((micros, 2)),
            dma((micros, sections, 2)), dma((micros, 2)),
            dma((3,)), dma((3,)), dma((3,)),
            dma((3,)), dma((3,)),
            dma((3,)), dma((3,)),
            dma((6,)), dma((6,)),
            dma((3,)),
        ],
        compiler_params=pltpu.CompilerParams(
            collective_id=0, has_side_effects=True, vmem_limit_bytes=60 * 1024 * 1024
        ),
        name="relay",
    )(
        tokens[:, 0, 0],
        regions[0],
        norm_gain,
        jnp.transpose(qkv_weight[0], (1, 0, 2)),
        out_weight[0],
        final_gain[None],
        jnp.transpose(dec_weight),
    )
    return decoded[:, None, None]


def solution(mesh):
    sizes = mesh.shape
    return jax.shard_map(
        functools.partial(body, sizes["section"], sizes["win"], sizes["dp"]),
        mesh=mesh,
        in_specs=(
            P(None, "win", "dp", None, None),
            P("section", "win", None),
            P("section", None),
            P("section", None, None, "dp"),
            P("section", "dp", None),
            P(),
            P(None, "section"),
        ),
        out_specs=P(None, "win", "dp", None, "section"),
        check_vma=False,
    )
```

time: 233 us -> 124 us (0.53)
  the two profiles are of different devices: /device:TPU:0 before, /device:TPU:1 now
where the time goes in v1:
time: 124 us; the launch traced here: 123 us
  Pallas kernels  121 us (98%)
  local copies, waits for them, and re-layouts  2.89 us (2%)
    pallas_call x1, Pallas kernels, body(): pl.pallas_call(functools.partial(kernel, sections, windows, bands), out_s...  121 us

profile of v1, /device:TPU:1, one launch (start us, length us, event | category | flops | bytes accessed | tf_op | source)
XLA Modules:
  0.0 123.4 jit_solution(401537990590587864)
XLA Ops:
  0.0 1.3 %broadcast_in_dim.6.final_gain = f32[1,1536]{1,0:T(1,128)} reshape(f32[1536]{0:T(1024)} %param.12) | data formatting | bytes 12288 | tf_op jit(solution)/shard_map/broadcast_in_dim | solution.py:420
  1.3 120.5 %relay.1 = bf16[2,64,552]{2,1,0:T(8,128)(2,1)} custom-call(bf16[2,64,1536]{2,1,0:T(8,128)(2,1)} %bitcast.14, s32[1,256]{1,0:T(1,128)} %bitcast.15, f32[1,1536]{1,0:T(1,128)} %gain.1, bf16[3,1536,256]{2,1,0:T(8,128)(2,1)} %bitcast.10, bf16[256,1536]{1,0:T(8,128)(2,1)} %bitcast.12, f32[1,1536]{1,0:T(1,128)} %broadcast_in_dim.6.final_gain, ...), custom_call_target="tpu_custom_call" | custom-call | tf_op jit(solution)/shard_map/relay/pallas_call | solution.py:381
  121.8 1.6 %copy.10 = bf16[2,1,1,64,552]{4,3,2,1,0:T(8,128)(2,1)} copy(bf16[2,1,1,64,552]{4,3,2,1,0:T(8,128)(2,1)} %bitcast.13) | data formatting | bytes 282624

commit v2 on v1

--- a/solution.py
+++ b/solution.py
@@ -24,9 +24,9 @@
     sections, windows, bands,
     tokens, labels, gain, wqkv_hbm, wout_hbm, final_gain, wdec_hbm,
     decoded,
-    full, relay, normed, projected, wqkv, wout, wdec, bias, bstage, blend, hstage, fstage, final,
+    full, relay_a, relay_b, ahead, normed, projected, wqkv, wout, wdec, bias, bstage, blend, hstage, fstage, final,
     ag_send, ag_recv, a2a_send, a2a_recv, hid_send, hid_recv, fin_send, fin_recv,
-    rel_send, rel_recv, fwd_send, wz_send, wz_recv, wy_send, wy_recv, wc_send, wc_recv, load_sem,
+    rel_send, rel_recv, fwd_send, nx_send, nx_recv, nf_send, wz_send, wz_recv, wy_send, wy_recv, wc_send, wc_recv, load_sem,
 ):
     micros, quad, width = tokens.shape
     half = quad // 2
@@ -51,25 +51,43 @@
             device_id=device, device_id_type=MESH,
         )
 
-    def ag_copy(m, k):
-        return send(full.at[m, b], full.at[m, b], ag_send.at[m, k - 1],
-                    ag_recv.at[m, bands - k - 1], (s, w, band(k)))
-
-    def ag_arrival(m, k):
-        slot = full.at[m, band(k)]
-        return send(slot, slot, ag_send.at[m, k - 1], ag_recv.at[m, k - 1], (s, w, band(k)))
-
-    def relay_copy(k):
-        return send(relay.at[b], relay.at[b], rel_send.at[k - 1],
-                    rel_recv.at[bands - k - 1], (s, w, band(k)))
-
-    def relay_arrival(k):
-        slot = relay.at[band(k)]
-        return send(slot, slot, rel_send.at[k - 1], rel_recv.at[k - 1], (s, w, band(k)))
-
-    def forward_copy(k):
-        return send(relay.at[band(k)], full.at[1, band(k)], fwd_send.at[k - 1],
-                    ag_recv.at[1, k - 1], (0, w, b))
+    def part_of(m, slot, part):
+        return full.at[m, slot, pl.ds(half * part, half)]
+
+    def ag_copy(m, k, part):
+        slot = part_of(m, b, part)
+        return send(slot, slot, ag_send.at[m, k - 1],
+                    ag_recv.at[m, bands - k - 1, part], (s, w, band(k)))
+
+    def ag_arrival(m, k, part):
+        slot = part_of(m, band(k), part)
+        return send(slot, slot, ag_send.at[m, k - 1], ag_recv.at[m, k - 1, part], (s, w, band(k)))
+
+    def relay_copy(m, k):
+        slot = (relay_b if m else relay_a).at[b]
+        return send(slot, slot, rel_send.at[m, k - 1],
+                    rel_recv.at[m, bands - k - 1], (s, w, band(k)))
+
+    def relay_arrival(m, k):
+        slot = (relay_b if m else relay_a).at[band(k)]
+        return send(slot, slot, rel_send.at[m, k - 1], rel_recv.at[m, k - 1], (s, w, band(k)))
+
+    def forward_copy(m, k, part):
+        slot = relay_b.at[band(k), pl.ds(half * part, half)] if m else relay_a.at[band(k)]
+        return send(slot, part_of(m, band(k), part), fwd_send.at[m + part if m else 0, k - 1],
+                    ag_recv.at[m, k - 1, part], (0, w, b))
+
+    def ahead_copy(m, k):
+        return send(hstage.at[m, pl.ds(half, half)], ahead.at[m, b], nx_send.at[m, k - 1],
+                    nx_recv.at[m, bands - k - 1], (s, w, band(k)))
+
+    def ahead_arrival(m, k):
+        slot = ahead.at[m, band(k)]
+        return send(slot, slot, nx_send.at[m, k - 1], nx_recv.at[m, k - 1], (s, w, band(k)))
+
+    def ahead_forward(m, k):
+        return send(ahead.at[m, band(k)], part_of(m, band(k), 0), nf_send.at[m, k - 1],
+                    ag_recv.at[m, k - 1, 0], (s + 1, w, b))
 
     def a2a_copy(m, k):
         return send(bstage.at[m, band(k)], blend.at[m, b], a2a_send.at[m, k - 1],
@@ -155,24 +173,16 @@
 
     @pl.when(s == 1)
     def _():
-        relay[b] = tokens[1]
+        relay_a[b] = tokens[0, half:]
+        relay_b[b] = tokens[1]
 
     pl.semaphore_wait(barrier, len(partners))
 
     def start_gather(m):
-        @pl.when(s > 0)
-        def _():
-            for part in range(2):
-                hidden_arrival(m, part).wait_recv()
-
-        if m == 1:
-            @pl.when(s > 0)
-            def _():
-                for k in others:
-                    ag_copy(m, k).start()
-        else:
-            for k in others:
-                ag_copy(m, k).start()
+        hidden_arrival(m, 1).wait_recv()
+        for k in others:
+            ag_copy(m, k, 1).start()
+        hidden_arrival(m, 0).wait_recv()
 
     def start_weights():
         for k in others:
@@ -201,7 +211,8 @@
     def project(m):
         normalize_band(m, b)
         for k in others:
-            ag_arrival(m, k).wait_recv()
+            ag_arrival(m, k, 0).wait_recv()
+            ag_arrival(m, k, 1).wait_recv()
             normalize_band(m, band(k))
         if m == 0:
             load_qkv.wait()
@@ -257,12 +268,14 @@
 
         @pl.when(s < last)
         def _():
-            for part in range(2):
-                hidden_copy(m, part).start()
+            hidden_copy(m, 1).start()
+            for k in others:
+                ahead_copy(m, k).start()
+            hidden_copy(m, 0).start()
 
         @pl.when(s == last)
         def _():
-            fstage[m] = normalize(hstage[m], final_gain[...])
+            fstage[m] = normalize(hstage[m], final_gain[...].reshape(1, width))
             for to in range(sections):
                 final_copy(m, to, 1).start()
                 if to != last:
@@ -279,55 +292,66 @@
             final[m], wdec[...], (((1,), (1,)), ((), ())), preferred_element_type=jnp.float32
         ).astype(jnp.bfloat16)
 
-    @pl.when(s == 1)
-    def _():
-        for k in others:
-            relay_copy(k).start()
-
-    @pl.when(s > 0)
-    def _():
-        start_weights()
-
     row = labels[...].astype(jnp.float32)
     across = jnp.broadcast_to(row, bias.shape)
+
+    @pl.when(s == 0)
+    def _():
+        start_weights()
+
+    @pl.when(s == 1)
+    def _():
+        for k in others:
+            relay_copy(0, k).start()
+
     bias[...] = jnp.where(across == across.T, 0.0, EXCLUDED)
 
     @pl.when(s == 1)
     def _():
         for k in others:
-            relay_arrival(k).wait_recv()
-            forward_copy(k).start()
+            relay_arrival(0, k).wait_recv()
+            forward_copy(0, k, 1).start()
+            if k == 1:
+                for to in others:
+                    relay_copy(1, to).start()
+        for k in others:
+            relay_arrival(1, k).wait_recv()
+            forward_copy(1, k, 0).start()
+            forward_copy(1, k, 1).start()
 
     @pl.when(s > 0)
     def _():
-        weights_over_chips()
-        weights_over_cores()
-
-    start_gather(0)
+        start_weights()
+
+    weights_over_chips()
 
     @pl.when(s == 0)
     def _():
-        start_weights()
+        for k in others:
+            ag_copy(0, k, 0).start()
+
+    @pl.when(s > 0)
+    def _():
+        for m in range(micros):
+            start_gather(m)
 
     project(0)
-    start_gather(1)
-
-    @pl.when(s == 0)
-    def _():
-        weights_over_chips()
-
     attend(0)
-
-    @pl.when(s == 0)
-    def _():
-        weights_over_cores()
-
+    weights_over_cores()
+    project(1)
+    attend(1)
     load_out.wait()
     weights_all()
     finish(0)
-    project(1)
-    attend(1)
     finish(1)
+
+    @pl.when(s < last)
+    def _():
+        for m in range(micros):
+            for k in others:
+                ahead_arrival(m, k).wait_recv()
+                ahead_forward(m, k).start()
+
     load_dec.wait()
     decode(0)
     decode(1)
@@ -335,30 +359,40 @@
     for m in range(micros):
         for k in others:
             a2a_copy(m, k).wait_send()
-            if m != 1:
-                ag_copy(m, k).wait_send()
     for k in others:
         wz_copy(k).wait_send()
         wy_copy(k).wait_send()
         wc_copy(k, 0).wait_send()
         wc_copy(k, 1).wait_send()
 
+    @pl.when(s == 0)
+    def _():
+        for k in others:
+            ag_copy(0, k, 0).wait_send()
+
     @pl.when(s > 0)
     def _():
-        for k in others:
-            ag_copy(1, k).wait_send()
+        for m in range(micros):
+            for k in others:
+                ag_copy(m, k, 1).wait_send()
 
     @pl.when(s == 1)
     def _():
         for k in others:
-            relay_copy(k).wait_send()
-            forward_copy(k).wait_send()
+            relay_copy(0, k).wait_send()
+            relay_copy(1, k).wait_send()
+            forward_copy(0, k, 1).wait_send()
+            forward_copy(1, k, 0).wait_send()
+            forward_copy(1, k, 1).wait_send()
 
     @pl.when(s < last)
     def _():
         for m in range(micros):
             for part in range(2):
                 hidden_copy(m, part).wait_send()
+            for k in others:
+                ahead_copy(m, k).wait_send()
+                ahead_forward(m, k).wait_send()
 
     @pl.when(s == last)
     def _():
@@ -385,7 +419,9 @@
         out_specs=vmem,
         scratch_shapes=[
             pltpu.VMEM((micros, bands, quad, width), bf16),
+            pltpu.VMEM((bands, quad // 2, width), bf16),
             pltpu.VMEM((bands, quad, width), bf16),
+            pltpu.VMEM((micros, bands, quad // 2, width), bf16),
             pltpu.VMEM((rows, width), bf16),
             pltpu.VMEM((3, rows, inner), bf16),
             pltpu.VMEM((3, width, inner), bf16),
@@ -397,11 +433,12 @@
             pltpu.VMEM((micros, quad, width), bf16),
             pltpu.VMEM((micros, quad, width), bf16),
             pltpu.VMEM((micros, quad, width), bf16),
-            dma((micros, 3)), dma((micros, 3)),
+            dma((micros, 3)), dma((micros, 3, 2)),
             dma((micros, 3)), dma((micros, 3)),
             dma((micros, 2)), dma((micros, 2)),
             dma((micros, sections, 2)), dma((micros, 2)),
-            dma((3,)), dma((3,)), dma((3,)),
+            dma((2, 3)), dma((2, 3)), dma((3, 3)),
+            dma((micros, 3)), dma((micros, 3)), dma((micros, 3)),
             dma((3,)), dma((3,)),
             dma((3,)), dma((3,)),
             dma((6,)), dma((6,)),
@@ -417,7 +454,7 @@
         norm_gain,
         jnp.transpose(qkv_weight[0], (1, 0, 2)),
         out_weight[0],
-        final_gain[None],
+        final_gain,
         jnp.transpose(dec_weight),
     )
     return decoded[:, None, None]

time: 124 us -> 91.7 us (0.74)
  the two profiles are of different devices: /device:TPU:1 before, /device:TPU:0 now
where the time goes in v2:
time: 91.7 us; the launch traced here: 91.5 us
  Pallas kernels  89.9 us (98%)
  local copies, waits for them, and re-layouts  1.6 us (2%)
    pallas_call x1, Pallas kernels, body(): pl.pallas_call(functools.partial(kernel, sections, windows, bands), out_s...  89.9 us

profile of v2, /device:TPU:0, one launch (start us, length us, event | category | flops | bytes accessed | tf_op | source)
XLA Modules:
  0.0 91.5 jit_solution(7681353333732384243)
XLA Ops:
  0.0 89.9 %relay.1 = bf16[2,64,552]{2,1,0:T(8,128)(2,1)} custom-call(bf16[2,64,1536]{2,1,0:T(8,128)(2,1)} %bitcast.14, s32[1,256]{1,0:T(1,128)} %bitcast.15, f32[1,1536]{1,0:T(1,128)} %gain.1, bf16[3,1536,256]{2,1,0:T(8,128)(2,1)} %bitcast.10, bf16[256,1536]{1,0:T(8,128)(2,1)} %bitcast.12, f32[1536]{0:T(1024)} %final_gain.1, bf16[552,1536]{1,0:T(8,128)(2,1)} %bitcast.11), custom_call_target="tpu_custom_call" | custom-call | tf_op jit(solution)/shard_map/relay/pallas_call | solution.py:415
  89.9 1.6 %copy.10 = bf16[2,1,1,64,552]{4,3,2,1,0:T(8,128)(2,1)} copy(bf16[2,1,1,64,552]{4,3,2,1,0:T(8,128)(2,1)} %bitcast.13) | data formatting | bytes 282624

commit v3 on v2

--- a/solution.py
+++ b/solution.py
@@ -26,7 +26,7 @@
     decoded,
     full, relay_a, relay_b, ahead, normed, projected, wqkv, wout, wdec, bias, bstage, blend, hstage, fstage, final,
     ag_send, ag_recv, a2a_send, a2a_recv, hid_send, hid_recv, fin_send, fin_recv,
-    rel_send, rel_recv, fwd_send, nx_send, nx_recv, nf_send, wz_send, wz_recv, wy_send, wy_recv, wc_send, wc_recv, load_sem,
+    chain_send, chain_recv, fwd_send, nx_send, nx_recv, nf_send, wy_send, wy_recv, wc_send, wc_recv, load_sem,
 ):
     micros, quad, width = tokens.shape
     half = quad // 2
@@ -40,7 +40,7 @@
     chip_peer = w + 2 - 4 * lax.rem(w // 2, 2)
     quarter = lax.rem(w, 4)
     group_rows = wout_hbm.shape[0]
-    piece = group_rows // 4
+    piece = group_rows // 8
 
     def band(k):
         return lax.rem(b + k, bands)
@@ -63,14 +63,54 @@
         slot = part_of(m, band(k), part)
         return send(slot, slot, ag_send.at[m, k - 1], ag_recv.at[m, k - 1, part], (s, w, band(k)))
 
-    def relay_copy(m, k):
-        slot = (relay_b if m else relay_a).at[b]
-        return send(slot, slot, rel_send.at[m, k - 1],
-                    rel_recv.at[m, bands - k - 1], (s, w, band(k)))
-
-    def relay_arrival(m, k):
-        slot = (relay_b if m else relay_a).at[band(k)]
-        return send(slot, slot, rel_send.at[m, k - 1], rel_recv.at[m, k - 1], (s, w, band(k)))
+    class Chain:
+        def __init__(self, index, slot, arrived):
+            self.index, self.slot, self.arrived = index, slot, arrived
+
+        def copy(self, way, distance, source):
+            slot = self.slot(source)
+            step = -1 if way else 1
+            return send(slot, slot, chain_send.at[self.index, way, distance],
+                        chain_recv.at[self.index, way, distance], (s, w, b + step))
+
+        def each(self, distance, do):
+            @pl.when((b >= distance) & (b < bands - 1))
+            def _():
+                do(self.copy(0, distance, b - distance))
+
+            @pl.when((b + distance < bands) & (b > 0))
+            def _():
+                do(self.copy(1, distance, b + distance))
+
+        def start(self):
+            self.each(0, lambda copy: copy.start())
+
+        def serve(self, distance):
+            @pl.when(b >= distance)
+            def _():
+                self.copy(0, distance - 1, b - distance).wait_recv()
+
+                if distance < bands - 1:
+                    @pl.when(b < bands - 1)
+                    def _():
+                        self.copy(0, distance, b - distance).start()
+
+                self.arrived(bands - distance)
+
+            @pl.when(b + distance < bands)
+            def _():
+                self.copy(1, distance - 1, b + distance).wait_recv()
+
+                if distance < bands - 1:
+                    @pl.when(b > 0)
+                    def _():
+                        self.copy(1, distance, b + distance).start()
+
+                self.arrived(distance)
+
+        def drain(self):
+            for distance in range(bands - 1):
+                self.each(distance, lambda copy: copy.wait_send())
 
     def forward_copy(m, k, part):
         slot = relay_b.at[band(k), pl.ds(half * part, half)] if m else relay_a.at[band(k)]
@@ -97,36 +137,28 @@
         slot = blend.at[m, band(k)]
         return send(slot, slot, a2a_send.at[m, k - 1], a2a_recv.at[m, k - 1], (s, w, band(k)))
 
-    def wz_copy(k):
-        rows = pl.ds(pl.multiple_of(quarter * piece, piece), piece)
-        return send(wout_hbm.at[rows], wout.at[b, rows], wz_send.at[k - 1],
-                    wz_recv.at[bands - k - 1], (s, w, band(k)))
-
-    def w_piece(k, owner):
-        return wout.at[band(k), pl.ds(pl.multiple_of(lax.rem(owner, 4) * piece, piece), piece)]
-
-    def wz_arrival(k):
-        slot = w_piece(k, w)
-        return send(slot, slot, wz_send.at[k - 1], wz_recv.at[k - 1], (s, w, band(k)))
-
-    def wy_copy(k):
-        slot = w_piece(k, w)
-        return send(slot, slot, wy_send.at[k - 1], wy_recv.at[k - 1], (s, chip_peer, b))
-
-    def wy_arrival(k):
-        slot = w_piece(k, chip_peer)
-        return send(slot, slot, wy_send.at[k - 1], wy_recv.at[k - 1], (s, chip_peer, b))
-
-    def wc_copy(k, far):
-        slot = w_piece(k, chip_peer if far else w)
+    def w_piece(slot, owner, chunk):
+        start = (lax.rem(owner, 4) * 2 + chunk) * piece
+        return wout.at[slot, pl.ds(pl.multiple_of(start, piece), piece)]
+
+    def wy_copy(k, chunk):
+        slot = w_piece(band(k), w, chunk)
+        return send(slot, slot, wy_send.at[chunk, k - 1], wy_recv.at[chunk, k - 1], (s, chip_peer, b))
+
+    def wy_arrival(k, chunk):
+        slot = w_piece(band(k), chip_peer, chunk)
+        return send(slot, slot, wy_send.at[chunk, k - 1], wy_recv.at[chunk, k - 1], (s, chip_peer, b))
+
+    def wc_copy(k, far, chunk):
+        slot = w_piece(band(k), chip_peer if far else w, chunk)
         index = 3 * far + k - 1
-        return send(slot, slot, wc_send.at[index], wc_recv.at[index], (s, core_peer, b))
-
-    def wc_arrival(k, far):
+        return send(slot, slot, wc_send.at[chunk, index], wc_recv.at[chunk, index], (s, core_peer, b))
+
+    def wc_arrival(k, far, chunk):
         other = core_peer + 2 - 4 * lax.rem(core_peer // 2, 2)
-        slot = w_piece(k, other if far else core_peer)
+        slot = w_piece(band(k), other if far else core_peer, chunk)
         index = 3 * far + k - 1
-        return send(slot, slot, wc_send.at[index], wc_recv.at[index], (s, core_peer, b))
+        return send(slot, slot, wc_send.at[chunk, index], wc_recv.at[chunk, index], (s, core_peer, b))
 
     def hidden_copy(m, part):
         rows_from = pl.ds(half * (1 - part), half)
@@ -149,6 +181,26 @@
         return send(slot, slot, fin_send.at[m, 0, part], fin_recv.at[m, part], (s, after, b))
 
     others = range(1, bands)
+    chunks = range(2)
+
+    def weights_arrived(chunk):
+        def arrived(k):
+            wy_copy(k, chunk).start()
+            wc_copy(k, 0, chunk).start()
+        return arrived
+
+    def relayed(m, part):
+        return lambda k: forward_copy(m, k, part).start()
+
+    first_half = Chain(0, lambda slot: part_of(0, slot, 0), lambda k: None)
+    relay_first = Chain(0, lambda slot: relay_a.at[slot], relayed(0, 1))
+    weight_chains = [
+        Chain(1 + c, lambda slot, c=c: w_piece(slot, w, c), weights_arrived(c)) for c in chunks
+    ]
+    relay_second = [
+        Chain(3 + c, lambda slot, c=c: relay_b.at[slot, pl.ds(half * c, half)], relayed(1, c))
+        for c in chunks
+    ]
 
     load_qkv = pltpu.make_async_copy(wqkv_hbm, wqkv, load_sem.at[0])
     load_out = pltpu.make_async_copy(wout_hbm, wout.at[b], load_sem.at[1])
@@ -184,25 +236,17 @@
             ag_copy(m, k, 1).start()
         hidden_arrival(m, 0).wait_recv()
 
-    def start_weights():
-        for k in others:
-            wz_copy(k).start()
-
-    def weights_over_chips():
-        for k in others:
-            wz_arrival(k).wait_recv()
-            wy_copy(k).start()
-            wc_copy(k, 0).start()
-
     def weights_over_cores():
         for k in others:
-            wy_arrival(k).wait_recv()
-            wc_copy(k, 1).start()
+            for chunk in chunks:
+                wy_arrival(k, chunk).wait_recv()
+                wc_copy(k, 1, chunk).start()
 
     def weights_all():
         for k in others:
-            wc_arrival(k, 0).wait_recv()
-            wc_arrival(k, 1).wait_recv()
+            for chunk in chunks:
+                wc_arrival(k, 0, chunk).wait_recv()
+                wc_arrival(k, 1, chunk).wait_recv()
 
     def normalize_band(m, slot):
         rows = pl.ds(pl.multiple_of(slot * quad, quad), quad)
@@ -211,7 +255,12 @@
     def project(m):
         normalize_band(m, b)
         for k in others:
-            ag_arrival(m, k, 0).wait_recv()
+            if m == 0:
+                @pl.when(s > 0)
+                def _():
+                    ag_arrival(m, k, 0).wait_recv()
+            else:
+                ag_arrival(m, k, 0).wait_recv()
             ag_arrival(m, k, 1).wait_recv()
             normalize_band(m, band(k))
         if m == 0:
@@ -295,63 +344,83 @@
     row = labels[...].astype(jnp.float32)
     across = jnp.broadcast_to(row, bias.shape)
 
+    load_out.wait()
+
     @pl.when(s == 0)
     def _():
-        start_weights()
+        for chain in weight_chains:
+            chain.start()
 
     @pl.when(s == 1)
     def _():
-        for k in others:
-            relay_copy(0, k).start()
+        relay_first.start()
 
     bias[...] = jnp.where(across == across.T, 0.0, EXCLUDED)
 
     @pl.when(s == 1)
     def _():
-        for k in others:
-            relay_arrival(0, k).wait_recv()
-            forward_copy(0, k, 1).start()
-            if k == 1:
-                for to in others:
-                    relay_copy(1, to).start()
-        for k in others:
-            relay_arrival(1, k).wait_recv()
-            forward_copy(1, k, 0).start()
-            forward_copy(1, k, 1).start()
-
-    @pl.when(s > 0)
-    def _():
-        start_weights()
-
-    weights_over_chips()
+        relay_first.serve(1)
+        relay_second[0].start()
+        relay_first.serve(2)
+        relay_second[1].start()
+        relay_first.serve(3)
+        for distance in others:
+            for chain in relay_second:
+                chain.serve(distance)
+            if distance == 2:
+                for chain in weight_chains:
+                    chain.start()
+
+    @pl.when(s > 1)
+    def _():
+        for chain in weight_chains:
+            chain.start()
+
+    for distance in others:
+        for chain in weight_chains:
+            chain.serve(distance)
+        if distance == 2:
+            @pl.when(s == 0)
+            def _():
+                first_half.start()
 
     @pl.when(s == 0)
     def _():
-        for k in others:
-            ag_copy(0, k, 0).start()
+        for distance in others:
+            first_half.serve(distance)
+        weights_over_cores()
 
     @pl.when(s > 0)
     def _():
         for m in range(micros):
             start_gather(m)
-
-    project(0)
-    attend(0)
-    weights_over_cores()
-    project(1)
-    attend(1)
-    load_out.wait()
-    weights_all()
-    finish(0)
-    finish(1)
-
-    @pl.when(s < last)
-    def _():
-        for m in range(micros):
+        weights_over_cores()
+
+    def hand_over(m):
+        @pl.when(s < last)
+        def _():
             for k in others:
                 ahead_arrival(m, k).wait_recv()
                 ahead_forward(m, k).start()
 
+    project(0)
+    attend(0)
+    weights_all()
+    project(1)
+
+    @pl.when(s < last)
+    def _():
+        finish(0)
+
+    attend(1)
+
+    @pl.when(s == last)
+    def _():
+        finish(0)
+
+    hand_over(0)
+    finish(1)
+    hand_over(1)
     load_dec.wait()
     decode(0)
     decode(1)
@@ -359,16 +428,17 @@
     for m in range(micros):
         for k in others:
             a2a_copy(m, k).wait_send()
+    for chain in weight_chains:
+        chain.drain()
     for k in others:
-        wz_copy(k).wait_send()
-        wy_copy(k).wait_send()
-        wc_copy(k, 0).wait_send()
-        wc_copy(k, 1).wait_send()
+        for chunk in chunks:
+            wy_copy(k, chunk).wait_send()
+            wc_copy(k, 0, chunk).wait_send()
+            wc_copy(k, 1, chunk).wait_send()
 
     @pl.when(s == 0)
     def _():
-        for k in others:
-            ag_copy(0, k, 0).wait_send()
+        first_half.drain()
 
     @pl.when(s > 0)
     def _():
@@ -378,9 +448,9 @@
 
     @pl.when(s == 1)
     def _():
-        for k in others:
-            relay_copy(0, k).wait_send()
-            relay_copy(1, k).wait_send()
+        for chain in [relay_first, *relay_second]:
+            chain.drain()
+        for k in others:
             forward_copy(0, k, 1).wait_send()
             forward_copy(1, k, 0).wait_send()
             forward_copy(1, k, 1).wait_send()
@@ -437,11 +507,10 @@
             dma((micros, 3)), dma((micros, 3)),
             dma((micros, 2)), dma((micros, 2)),
             dma((micros, sections, 2)), dma((micros, 2)),
-            dma((2, 3)), dma((2, 3)), dma((3, 3)),
+            dma((5, 2, 3)), dma((5, 2, 3)), dma((3, 3)),
             dma((micros, 3)), dma((micros, 3)), dma((micros, 3)),
-            dma((3,)), dma((3,)),
-            dma((3,)), dma((3,)),
-            dma((6,)), dma((6,)),
+            dma((2, 3)), dma((2, 3)),
+            dma((2, 6)), dma((2, 6)),
             dma((3,)),
         ],
         compiler_params=pltpu.CompilerParams(

time: 91.7 us -> 79.7 us (0.87)
  Pallas kernels: 89.9 us -> 77.5 us
    pallas_call x1, Pallas kernels: 89.9 us -> 77.5 us  [body(): pl.pallas_call(functools.partial(kernel, sections, windows, bands), out_s...]
where the time goes in v3:
time: 79.7 us; the launch traced here: 79.1 us
  Pallas kernels  77.5 us (97%)
  local copies, waits for them, and re-layouts  1.6 us (2%)
    pallas_call x1, Pallas kernels, body(): pl.pallas_call(functools.partial(kernel, sections, windows, bands), out_s...  77.5 us
    unnamed x1, local copies, waits for them, and re-layouts  1.6 us

profile of v3, /device:TPU:0, one launch (start us, length us, event | category | flops | bytes accessed | tf_op | source)
XLA Modules:
  0.0 79.1 jit_solution(14616885231762480298)
XLA Ops:
  0.0 77.5 %relay.1 = bf16[2,64,552]{2,1,0:T(8,128)(2,1)} custom-call(bf16[2,64,1536]{2,1,0:T(8,128)(2,1)} %bitcast.14, s32[1,256]{1,0:T(1,128)} %bitcast.15, f32[1,1536]{1,0:T(1,128)} %gain.1, bf16[3,1536,256]{2,1,0:T(8,128)(2,1)} %bitcast.10, bf16[256,1536]{1,0:T(8,128)(2,1)} %bitcast.12, f32[1536]{0:T(1024)} %final_gain.1, bf16[552,1536]{1,0:T(8,128)(2,1)} %bitcast.11), custom_call_target="tpu_custom_call" | custom-call | tf_op jit(solution)/shard_map/relay/pallas_call | solution.py:485
  77.5 1.6 %copy.10 = bf16[2,1,1,64,552]{4,3,2,1,0:T(8,128)(2,1)} copy(bf16[2,1,1,64,552]{4,3,2,1,0:T(8,128)(2,1)} %bitcast.13) | data formatting | bytes 282624

commit v4 on v3

--- a/solution.py
+++ b/solution.py
@@ -348,8 +348,7 @@
 
     @pl.when(s == 0)
     def _():
-        for chain in weight_chains:
-            chain.start()
+        first_half.start()
 
     @pl.when(s == 1)
     def _():
@@ -376,25 +375,24 @@
         for chain in weight_chains:
             chain.start()
 
-    for distance in others:
+    def serve_weights(distance):
         for chain in weight_chains:
             chain.serve(distance)
-        if distance == 2:
-            @pl.when(s == 0)
-            def _():
-                first_half.start()
 
     @pl.when(s == 0)
     def _():
+        first_half.serve(1)
+        for chain in weight_chains:
+            chain.start()
+        first_half.serve(2)
+        first_half.serve(3)
+
+    @pl.when(s > 0)
+    def _():
         for distance in others:
-            first_half.serve(distance)
-        weights_over_cores()
-
-    @pl.when(s > 0)
-    def _():
+            serve_weights(distance)
         for m in range(micros):
             start_gather(m)
-        weights_over_cores()
 
     def hand_over(m):
         @pl.when(s < last)
@@ -404,14 +402,26 @@
                 ahead_forward(m, k).start()
 
     project(0)
+
+    @pl.when(s == 0)
+    def _():
+        serve_weights(1)
+
     attend(0)
+
+    @pl.when(s == 0)
+    def _():
+        serve_weights(2)
+        serve_weights(3)
+
+    weights_over_cores()
     weights_all()
+
+    @pl.when(s < last)
+    def _():
+        finish(0)
+
     project(1)
-
-    @pl.when(s < last)
-    def _():
-        finish(0)
-
     attend(1)
 
     @pl.when(s == last)

time: 79.7 us -> 83.3 us (1.045)
  Pallas kernels: 77.5 us -> 81.5 us
    pallas_call x1, Pallas kernels: 77.5 us -> 81.5 us  [body(): pl.pallas_call(functools.partial(kernel, sections, windows, bands), out_s...]
where the time goes in v4:
time: 83.3 us; the launch traced here: 83.1 us
  Pallas kernels  81.5 us (98%)
  local copies, waits for them, and re-layouts  1.6 us (2%)
    pallas_call x1, Pallas kernels, body(): pl.pallas_call(functools.partial(kernel, sections, windows, bands), out_s...  81.5 us

profile of v4, /device:TPU:0, one launch (start us, length us, event | category | flops | bytes accessed | tf_op | source)
XLA Modules:
  0.0 83.1 jit_solution(1635266863223918703)
XLA Ops:
  0.0 81.5 %relay.1 = bf16[2,64,552]{2,1,0:T(8,128)(2,1)} custom-call(bf16[2,64,1536]{2,1,0:T(8,128)(2,1)} %bitcast.14, s32[1,256]{1,0:T(1,128)} %bitcast.15, f32[1,1536]{1,0:T(1,128)} %gain.1, bf16[3,1536,256]{2,1,0:T(8,128)(2,1)} %bitcast.10, bf16[256,1536]{1,0:T(8,128)(2,1)} %bitcast.12, f32[1536]{0:T(1024)} %final_gain.1, bf16[552,1536]{1,0:T(8,128)(2,1)} %bitcast.11), custom_call_target="tpu_custom_call" | custom-call | tf_op jit(solution)/shard_map/relay/pallas_call | solution.py:495
  81.5 1.6 %copy.10 = bf16[2,1,1,64,552]{4,3,2,1,0:T(8,128)(2,1)} copy(bf16[2,1,1,64,552]{4,3,2,1,0:T(8,128)(2,1)} %bitcast.13) | data formatting | bytes 282624

commit v5 on v3

--- a/solution.py
+++ b/solution.py
@@ -11,6 +11,7 @@
 HEAD_DIM = 64
 MESH = pl.DeviceIdType.MESH
 EXCLUDED = -1e30
+QUARTERS_AHEAD = (2, 1)
 
 
 def normalize(hidden, scales):
@@ -25,8 +26,8 @@
     tokens, labels, gain, wqkv_hbm, wout_hbm, final_gain, wdec_hbm,
     decoded,
     full, relay_a, relay_b, ahead, normed, projected, wqkv, wout, wdec, bias, bstage, blend, hstage, fstage, final,
-    ag_send, ag_recv, a2a_send, a2a_recv, hid_send, hid_recv, fin_send, fin_recv,
-    chain_send, chain_recv, fwd_send, nx_send, nx_recv, nf_send, wy_send, wy_recv, wc_send, wc_recv, load_sem,
+    ag_recv, a2a_send, a2a_recv, hid_send, hid_recv, fin_send, fin_recv,
+    chain_send, chain_recv, fwd_send, nf_send, wy_send, wy_recv, wc_send, wc_recv, load_sem,
 ):
     micros, quad, width = tokens.shape
     half = quad // 2
@@ -54,14 +55,16 @@
     def part_of(m, slot, part):
         return full.at[m, slot, pl.ds(half * part, half)]
 
-    def ag_copy(m, k, part):
-        slot = part_of(m, b, part)
-        return send(slot, slot, ag_send.at[m, k - 1],
-                    ag_recv.at[m, bands - k - 1, part], (s, w, band(k)))
-
-    def ag_arrival(m, k, part):
+    def quarter_of(m, slot, q):
+        return full.at[m, slot, pl.ds(half // 2 * q, half // 2)]
+
+    def part_arrival(m, k, part):
         slot = part_of(m, band(k), part)
-        return send(slot, slot, ag_send.at[m, k - 1], ag_recv.at[m, k - 1, part], (s, w, band(k)))
+        return send(slot, slot, fwd_send.at[0, k - 1], ag_recv.at[m, k - 1, 2 * part], (s, w, band(k)))
+
+    def quarter_arrival(m, k, q):
+        slot = quarter_of(m, band(k), q)
+        return send(slot, slot, fwd_send.at[0, k - 1], ag_recv.at[m, k - 1, q], (s, w, band(k)))
 
     class Chain:
         def __init__(self, index, slot, arrived):
@@ -115,19 +118,12 @@
     def forward_copy(m, k, part):
         slot = relay_b.at[band(k), pl.ds(half * part, half)] if m else relay_a.at[band(k)]
         return send(slot, part_of(m, band(k), part), fwd_send.at[m + part if m else 0, k - 1],
-                    ag_recv.at[m, k - 1, part], (0, w, b))
-
-    def ahead_copy(m, k):
-        return send(hstage.at[m, pl.ds(half, half)], ahead.at[m, b], nx_send.at[m, k - 1],
-                    nx_recv.at[m, bands - k - 1], (s, w, band(k)))
-
-    def ahead_arrival(m, k):
-        slot = ahead.at[m, band(k)]
-        return send(slot, slot, nx_send.at[m, k - 1], nx_recv.at[m, k - 1], (s, w, band(k)))
-
-    def ahead_forward(m, k):
-        return send(ahead.at[m, band(k)], part_of(m, band(k), 0), nf_send.at[m, k - 1],
-                    ag_recv.at[m, k - 1, 0], (s + 1, w, b))
+                    ag_recv.at[m, k - 1, 2 * part], (0, w, b))
+
+    def ahead_forward(m, k, q):
+        rows = pl.ds(half // 2 * q, half // 2)
+        return send(ahead.at[m, band(k), rows], quarter_of(m, band(k), q), nf_send.at[m, k - 1, q],
+                    ag_recv.at[m, k - 1, q], (s + 1, w, b))
 
     def a2a_copy(m, k):
         return send(bstage.at[m, band(k)], blend.at[m, b], a2a_send.at[m, k - 1],
@@ -182,6 +178,23 @@
 
     others = range(1, bands)
     chunks = range(2)
+
+    gather_chains = [
+        [
+            Chain(5 + 4 * m + q, lambda slot, m=m, q=q: quarter_of(m, slot, q), lambda k: None)
+            for q in (2, 3, 1, 0)[:4 - QUARTERS_AHEAD[m]]
+        ]
+        for m in range(micros)
+    ]
+    ahead_chains = [
+        [
+            Chain(13 + 2 * m + q,
+                  lambda slot, m=m, q=q: ahead.at[m, slot, pl.ds(half // 2 * q, half // 2)],
+                  lambda k, m=m, q=q: ahead_forward(m, k, q).start())
+            for q in range(QUARTERS_AHEAD[m])
+        ]
+        for m in range(micros)
+    ]
 
     def weights_arrived(chunk):
         def arrived(k):
@@ -232,9 +245,15 @@
 
     def start_gather(m):
         hidden_arrival(m, 1).wait_recv()
-        for k in others:
-            ag_copy(m, k, 1).start()
+        for chain in gather_chains[m][:2]:
+            chain.start()
         hidden_arrival(m, 0).wait_recv()
+        for chain in gather_chains[m][2:]:
+            chain.start()
+
+    def serve_gather(m, distance):
+        for chain in gather_chains[m]:
+            chain.serve(distance)
 
     def weights_over_cores():
         for k in others:
@@ -255,13 +274,17 @@
     def project(m):
         normalize_band(m, b)
         for k in others:
-            if m == 0:
-                @pl.when(s > 0)
-                def _():
-                    ag_arrival(m, k, 0).wait_recv()
-            else:
-                ag_arrival(m, k, 0).wait_recv()
-            ag_arrival(m, k, 1).wait_recv()
+            @pl.when(s == 0)
+            def _():
+                for part in range(2):
+                    if m + part > 0:
+                        part_arrival(m, k, part).wait_recv()
+
+            @pl.when(s > 0)
+            def _():
+                for q in range(QUARTERS_AHEAD[m]):
+                    quarter_arrival(m, k, q).wait_recv()
+
             normalize_band(m, band(k))
         if m == 0:
             load_qkv.wait()
@@ -318,8 +341,9 @@
         @pl.when(s < last)
         def _():
             hidden_copy(m, 1).start()
-            for k in others:
-                ahead_copy(m, k).start()
+            ahead[m, b] = hstage[m, half:]
+            for chain in ahead_chains[m]:
+                chain.start()
             hidden_copy(m, 0).start()
 
         @pl.when(s == last)
@@ -392,19 +416,33 @@
 
     @pl.when(s > 0)
     def _():
-        for m in range(micros):
-            start_gather(m)
+        start_gather(0)
+        serve_gather(0, 1)
+        serve_gather(0, 2)
         weights_over_cores()
+        start_gather(1)
+        serve_gather(0, 3)
 
     def hand_over(m):
         @pl.when(s < last)
         def _():
-            for k in others:
-                ahead_arrival(m, k).wait_recv()
-                ahead_forward(m, k).start()
+            for distance in others:
+                for chain in ahead_chains[m]:
+                    chain.serve(distance)
 
     project(0)
+
+    @pl.when(s > 0)
+    def _():
+        serve_gather(1, 1)
+
     attend(0)
+
+    @pl.when(s > 0)
+    def _():
+        serve_gather(1, 2)
+        serve_gather(1, 3)
+
     weights_all()
     project(1)
 
@@ -442,9 +480,8 @@
 
     @pl.when(s > 0)
     def _():
-        for m in range(micros):
-            for k in others:
-                ag_copy(m, k, 1).wait_send()
+        for chain in gather_chains[0] + gather_chains[1]:
+            chain.drain()
 
     @pl.when(s == 1)
     def _():
@@ -460,9 +497,11 @@
         for m in range(micros):
             for part in range(2):
                 hidden_copy(m, part).wait_send()
+            for chain in ahead_chains[m]:
+                chain.drain()
             for k in others:
-                ahead_copy(m, k).wait_send()
-                ahead_forward(m, k).wait_send()
+                for q in range(QUARTERS_AHEAD[m]):
+                    ahead_forward(m, k, q).wait_send()
 
     @pl.when(s == last)
     def _():
@@ -503,12 +542,12 @@
             pltpu.VMEM((micros, quad, width), bf16),
             pltpu.VMEM((micros, quad, width), bf16),
             pltpu.VMEM((micros, quad, width), bf16),
-            dma((micros, 3)), dma((micros, 3, 2)),
+            dma((micros, 3, 4)),
             dma((micros, 3)), dma((micros, 3)),
             dma((micros, 2)), dma((micros, 2)),
             dma((micros, sections, 2)), dma((micros, 2)),
-            dma((5, 2, 3)), dma((5, 2, 3)), dma((3, 3)),
-            dma((micros, 3)), dma((micros, 3)), dma((micros, 3)),
+            dma((17, 2, 3)), dma((17, 2, 3)), dma((3, 3)),
+            dma((micros, 3, 2)),
             dma((2, 3)), dma((2, 3)),
             dma((2, 6)), dma((2, 6)),
             dma((3,)),

time: 79.7 us -> 83.9 us (1.053)
  Pallas kernels: 77.5 us -> 82.2 us
    pallas_call x1, Pallas kernels: 77.5 us -> 82.2 us  [body(): pl.pallas_call(functools.partial(kernel, sections, windows, bands), out_s...]
where the time goes in v5:
time: 83.9 us; the launch traced here: 83.8 us
  Pallas kernels  82.2 us (98%)
  local copies, waits for them, and re-layouts  1.6 us (2%)
    pallas_call x1, Pallas kernels, body(): pl.pallas_call(functools.partial(kernel, sections, windows, bands), out_s...  82.2 us

profile of v5, /device:TPU:0, one launch (start us, length us, event | category | flops | bytes accessed | tf_op | source)
XLA Modules:
  0.0 83.8 jit_solution(15400339902101769079)
XLA Ops:
  0.0 82.2 %relay.1 = bf16[2,64,552]{2,1,0:T(8,128)(2,1)} custom-call(bf16[2,64,1536]{2,1,0:T(8,128)(2,1)} %bitcast.14, s32[1,256]{1,0:T(1,128)} %bitcast.15, f32[1,1536]{1,0:T(1,128)} %gain.1, bf16[3,1536,256]{2,1,0:T(8,128)(2,1)} %bitcast.10, bf16[256,1536]{1,0:T(8,128)(2,1)} %bitcast.12, f32[1536]{0:T(1024)} %final_gain.1, bf16[552,1536]{1,0:T(8,128)(2,1)} %bitcast.11), custom_call_target="tpu_custom_call" | custom-call | tf_op jit(solution)/shard_map/relay/pallas_call | solution.py:524
  82.2 1.6 %copy.10 = bf16[2,1,1,64,552]{4,3,2,1,0:T(8,128)(2,1)} copy(bf16[2,1,1,64,552]{4,3,2,1,0:T(8,128)(2,1)} %bitcast.13) | data formatting | bytes 282624

commit v6 on v3

--- a/solution.py
+++ b/solution.py
@@ -418,8 +418,8 @@
     def _():
         finish(0)
 
+    finish(1)
     hand_over(0)
-    finish(1)
     hand_over(1)
     load_dec.wait()
     decode(0)

time: 79.7 us -> 80.9 us (1.015)
  Pallas kernels: 77.5 us -> 79.2 us
    pallas_call x1, Pallas kernels: 77.5 us -> 79.2 us  [body(): pl.pallas_call(functools.partial(kernel, sections, windows, bands), out_s...]
where the time goes in v6:
time: 80.9 us; the launch traced here: 80.8 us
  Pallas kernels  79.2 us (98%)
  local copies, waits for them, and re-layouts  1.6 us (2%)
    pallas_call x1, Pallas kernels, body(): pl.pallas_call(functools.partial(kernel, sections, windows, bands), out_s...  79.2 us

profile of v6, /device:TPU:0, one launch (start us, length us, event | category | flops | bytes accessed | tf_op | source)
XLA Modules:
  0.0 80.8 jit_solution(5028372284551304679)
XLA Ops:
  0.0 79.2 %relay.1 = bf16[2,64,552]{2,1,0:T(8,128)(2,1)} custom-call(bf16[2,64,1536]{2,1,0:T(8,128)(2,1)} %bitcast.14, s32[1,256]{1,0:T(1,128)} %bitcast.15, f32[1,1536]{1,0:T(1,128)} %gain.1, bf16[3,1536,256]{2,1,0:T(8,128)(2,1)} %bitcast.10, bf16[256,1536]{1,0:T(8,128)(2,1)} %bitcast.12, f32[1536]{0:T(1024)} %final_gain.1, bf16[552,1536]{1,0:T(8,128)(2,1)} %bitcast.11), custom_call_target="tpu_custom_call" | custom-call | tf_op jit(solution)/shard_map/relay/pallas_call | solution.py:485
  79.2 1.6 %copy.10 = bf16[2,1,1,64,552]{4,3,2,1,0:T(8,128)(2,1)} copy(bf16[2,1,1,64,552]{4,3,2,1,0:T(8,128)(2,1)} %bitcast.13) | data formatting | bytes 282624

commit v7 on v3

--- a/solution.py
+++ b/solution.py
@@ -348,7 +348,7 @@
 
     @pl.when(s == 0)
     def _():
-        for chain in weight_chains:
+        for chain in [first_half, *weight_chains]:
             chain.start()
 
     @pl.when(s == 1)
@@ -379,15 +379,13 @@
     for distance in others:
         for chain in weight_chains:
             chain.serve(distance)
-        if distance == 2:
-            @pl.when(s == 0)
-            def _():
-                first_half.start()
+
+        @pl.when(s == 0)
+        def _():
+            first_half.serve(distance)
 
     @pl.when(s == 0)
     def _():
-        for distance in others:
-            first_half.serve(distance)
         weights_over_cores()
 
     @pl.when(s > 0)

time: 79.7 us -> 79.4 us (level)
  no operation moved by 1% of the time
where the time goes in v7:
time: 79.4 us; the launch traced here: 79.2 us
  Pallas kernels  77.6 us (98%)
  local copies, waits for them, and re-layouts  1.6 us (2%)
    pallas_call x1, Pallas kernels, body(): pl.pallas_call(functools.partial(kernel, sections, windows, bands), out_s...  77.6 us
    unnamed x1, local copies, waits for them, and re-layouts  1.6 us

profile of v7, /device:TPU:0, one launch (start us, length us, event | category | flops | bytes accessed | tf_op | source)
XLA Modules:
  0.0 79.2 jit_solution(3488841084796817841)
XLA Ops:
  0.0 77.6 %relay.1 = bf16[2,64,552]{2,1,0:T(8,128)(2,1)} custom-call(bf16[2,64,1536]{2,1,0:T(8,128)(2,1)} %bitcast.14, s32[1,256]{1,0:T(1,128)} %bitcast.15, f32[1,1536]{1,0:T(1,128)} %gain.1, bf16[3,1536,256]{2,1,0:T(8,128)(2,1)} %bitcast.10, bf16[256,1536]{1,0:T(8,128)(2,1)} %bitcast.12, f32[1536]{0:T(1024)} %final_gain.1, bf16[552,1536]{1,0:T(8,128)(2,1)} %bitcast.11), custom_call_target="tpu_custom_call" | custom-call | tf_op jit(solution)/shard_map/relay/pallas_call | solution.py:483
  77.6 1.6 %copy.10 = bf16[2,1,1,64,552]{4,3,2,1,0:T(8,128)(2,1)} copy(bf16[2,1,1,64,552]{4,3,2,1,0:T(8,128)(2,1)} %bitcast.13) | data formatting | bytes 282624

commit v8 on v7

--- a/solution.py
+++ b/solution.py
@@ -384,10 +384,6 @@
         def _():
             first_half.serve(distance)
 
-    @pl.when(s == 0)
-    def _():
-        weights_over_cores()
-
     @pl.when(s > 0)
     def _():
         for m in range(micros):
@@ -403,6 +399,11 @@
 
     project(0)
     attend(0)
+
+    @pl.when(s == 0)
+    def _():
+        weights_over_cores()
+
     weights_all()
     project(1)
 

time: 79.4 us -> 79.5 us (level)
  no operation moved by 1% of the time
where the time goes in v8:
time: 79.5 us; the launch traced here: 79.4 us
  Pallas kernels  77.8 us (98%)
  local copies, waits for them, and re-layouts  1.6 us (2%)
    pallas_call x1, Pallas kernels, body(): pl.pallas_call(functools.partial(kernel, sections, windows, bands), out_s...  77.8 us
    unnamed x1, local copies, waits for them, and re-layouts  1.6 us

profile of v8, /device:TPU:0, one launch (start us, length us, event | category | flops | bytes accessed | tf_op | source)
XLA Modules:
  0.0 79.4 jit_solution(16314186276516013335)
XLA Ops:
  0.0 77.8 %relay.1 = bf16[2,64,552]{2,1,0:T(8,128)(2,1)} custom-call(bf16[2,64,1536]{2,1,0:T(8,128)(2,1)} %bitcast.14, s32[1,256]{1,0:T(1,128)} %bitcast.15, f32[1,1536]{1,0:T(1,128)} %gain.1, bf16[3,1536,256]{2,1,0:T(8,128)(2,1)} %bitcast.10, bf16[256,1536]{1,0:T(8,128)(2,1)} %bitcast.12, f32[1536]{0:T(1024)} %final_gain.1, bf16[552,1536]{1,0:T(8,128)(2,1)} %bitcast.11), custom_call_target="tpu_custom_call" | custom-call | tf_op jit(solution)/shard_map/relay/pallas_call | solution.py:484
  77.8 1.6 %copy.10 = bf16[2,1,1,64,552]{4,3,2,1,0:T(8,128)(2,1)} copy(bf16[2,1,1,64,552]{4,3,2,1,0:T(8,128)(2,1)} %bitcast.13) | data formatting | bytes 282624

commit v9 on v8

--- a/solution.py
+++ b/solution.py
@@ -112,10 +112,10 @@
             for distance in range(bands - 1):
                 self.each(distance, lambda copy: copy.wait_send())
 
-    def forward_copy(m, k, part):
-        slot = relay_b.at[band(k), pl.ds(half * part, half)] if m else relay_a.at[band(k)]
-        return send(slot, part_of(m, band(k), part), fwd_send.at[m + part if m else 0, k - 1],
-                    ag_recv.at[m, k - 1, part], (0, w, b))
+    def forward_copy(m, k):
+        slot = (relay_b if m else relay_a).at[band(k)]
+        return send(slot, part_of(m, band(k), 1), fwd_send.at[m, k - 1],
+                    ag_recv.at[m, k - 1, 1], (0, w, b))
 
     def ahead_copy(m, k):
         return send(hstage.at[m, pl.ds(half, half)], ahead.at[m, b], nx_send.at[m, k - 1],
@@ -189,17 +189,18 @@
             wc_copy(k, 0, chunk).start()
         return arrived
 
-    def relayed(m, part):
-        return lambda k: forward_copy(m, k, part).start()
-
-    first_half = Chain(0, lambda slot: part_of(0, slot, 0), lambda k: None)
-    relay_first = Chain(0, lambda slot: relay_a.at[slot], relayed(0, 1))
+    def relayed(m):
+        return lambda k: forward_copy(m, k).start()
+
+    own_halves = [
+        Chain(3 * m, lambda slot, m=m: part_of(m, slot, 0), lambda k: None) for m in range(2)
+    ]
+    relays = [
+        Chain(0, lambda slot: relay_a.at[slot], relayed(0)),
+        Chain(3, lambda slot: relay_b.at[slot], relayed(1)),
+    ]
     weight_chains = [
         Chain(1 + c, lambda slot, c=c: w_piece(slot, w, c), weights_arrived(c)) for c in chunks
-    ]
-    relay_second = [
-        Chain(3 + c, lambda slot, c=c: relay_b.at[slot, pl.ds(half * c, half)], relayed(1, c))
-        for c in chunks
     ]
 
     load_qkv = pltpu.make_async_copy(wqkv_hbm, wqkv, load_sem.at[0])
@@ -226,7 +227,7 @@
     @pl.when(s == 1)
     def _():
         relay_a[b] = tokens[0, half:]
-        relay_b[b] = tokens[1]
+        relay_b[b] = tokens[1, half:]
 
     pl.semaphore_wait(barrier, len(partners))
 
@@ -255,12 +256,10 @@
     def project(m):
         normalize_band(m, b)
         for k in others:
-            if m == 0:
-                @pl.when(s > 0)
-                def _():
-                    ag_arrival(m, k, 0).wait_recv()
-            else:
+            @pl.when(s > 0)
+            def _():
                 ag_arrival(m, k, 0).wait_recv()
+
             ag_arrival(m, k, 1).wait_recv()
             normalize_band(m, band(k))
         if m == 0:
@@ -348,24 +347,20 @@
 
     @pl.when(s == 0)
     def _():
-        for chain in [first_half, *weight_chains]:
+        for chain in [own_halves[0], *weight_chains]:
             chain.start()
 
     @pl.when(s == 1)
     def _():
-        relay_first.start()
+        for chain in relays:
+            chain.start()
 
     bias[...] = jnp.where(across == across.T, 0.0, EXCLUDED)
 
     @pl.when(s == 1)
     def _():
-        relay_first.serve(1)
-        relay_second[0].start()
-        relay_first.serve(2)
-        relay_second[1].start()
-        relay_first.serve(3)
         for distance in others:
-            for chain in relay_second:
+            for chain in relays:
                 chain.serve(distance)
             if distance == 2:
                 for chain in weight_chains:
@@ -382,7 +377,9 @@
 
         @pl.when(s == 0)
         def _():
-            first_half.serve(distance)
+            own_halves[0].serve(distance)
+            if distance == 2:
+                own_halves[1].start()
 
     @pl.when(s > 0)
     def _():
@@ -398,11 +395,18 @@
                 ahead_forward(m, k).start()
 
     project(0)
+
+    @pl.when(s == 0)
+    def _():
+        own_halves[1].serve(1)
+
     attend(0)
 
     @pl.when(s == 0)
     def _():
+        own_halves[1].serve(2)
         weights_over_cores()
+        own_halves[1].serve(3)
 
     weights_all()
     project(1)
@@ -437,7 +441,8 @@
 
     @pl.when(s == 0)
     def _():
-        first_half.drain()
+        for chain in own_halves:
+            chain.drain()
 
     @pl.when(s > 0)
     def _():
@@ -447,12 +452,11 @@
 
     @pl.when(s == 1)
     def _():
-        for chain in [relay_first, *relay_second]:
+        for chain in relays:
             chain.drain()
         for k in others:
-            forward_copy(0, k, 1).wait_send()
-            forward_copy(1, k, 0).wait_send()
-            forward_copy(1, k, 1).wait_send()
+            forward_copy(0, k).wait_send()
+            forward_copy(1, k).wait_send()
 
     @pl.when(s < last)
     def _():
@@ -489,7 +493,7 @@
         scratch_shapes=[
             pltpu.VMEM((micros, bands, quad, width), bf16),
             pltpu.VMEM((bands, quad // 2, width), bf16),
-            pltpu.VMEM((bands, quad, width), bf16),
+            pltpu.VMEM((bands, quad // 2, width), bf16),
             pltpu.VMEM((micros, bands, quad // 2, width), bf16),
             pltpu.VMEM((rows, width), bf16),
             pltpu.VMEM((3, rows, inner), bf16),
@@ -506,7 +510,7 @@
             dma((micros, 3)), dma((micros, 3)),
             dma((micros, 2)), dma((micros, 2)),
             dma((micros, sections, 2)), dma((micros, 2)),
-            dma((5, 2, 3)), dma((5, 2, 3)), dma((3, 3)),
+            dma((4, 2, 3)), dma((4, 2, 3)), dma((2, 3)),
             dma((micros, 3)), dma((micros, 3)), dma((micros, 3)),
             dma((2, 3)), dma((2, 3)),
             dma((2, 6)), dma((2, 6)),

time: 79.5 us -> 82.7 us (1.040)
  Pallas kernels: 77.8 us -> 80.3 us
    pallas_call x1, Pallas kernels: 77.8 us -> 80.3 us  [body(): pl.pallas_call(functools.partial(kernel, sections, windows, bands), out_s...]
where the time goes in v9:
time: 82.7 us; the launch traced here: 81.9 us
  Pallas kernels  80.3 us (97%)
  local copies, waits for them, and re-layouts  1.6 us (2%)
    pallas_call x1, Pallas kernels, body(): pl.pallas_call(functools.partial(kernel, sections, windows, bands), out_s...  80.3 us

profile of v9, /device:TPU:0, one launch (start us, length us, event | category | flops | bytes accessed | tf_op | source)
XLA Modules:
  0.0 81.9 jit_solution(11140992069562845242)
XLA Ops:
  0.0 80.3 %relay.1 = bf16[2,64,552]{2,1,0:T(8,128)(2,1)} custom-call(bf16[2,64,1536]{2,1,0:T(8,128)(2,1)} %bitcast.14, s32[1,256]{1,0:T(1,128)} %bitcast.15, f32[1,1536]{1,0:T(1,128)} %gain.1, bf16[3,1536,256]{2,1,0:T(8,128)(2,1)} %bitcast.10, bf16[256,1536]{1,0:T(8,128)(2,1)} %bitcast.12, f32[1536]{0:T(1024)} %final_gain.1, bf16[552,1536]{1,0:T(8,128)(2,1)} %bitcast.11), custom_call_target="tpu_custom_call" | custom-call | tf_op jit(solution)/shard_map/relay/pallas_call | solution.py:488
  80.3 1.6 %copy.10 = bf16[2,1,1,64,552]{4,3,2,1,0:T(8,128)(2,1)} copy(bf16[2,1,1,64,552]{4,3,2,1,0:T(8,128)(2,1)} %bitcast.13) | data formatting | bytes 282624

commit v10 on v8

--- a/solution.py
+++ b/solution.py
@@ -129,13 +129,17 @@
         return send(ahead.at[m, band(k)], part_of(m, band(k), 0), nf_send.at[m, k - 1],
                     ag_recv.at[m, k - 1, 0], (s + 1, w, b))
 
-    def a2a_copy(m, k):
-        return send(bstage.at[m, band(k)], blend.at[m, b], a2a_send.at[m, k - 1],
-                    a2a_recv.at[m, bands - k - 1], (s, w, band(k)))
-
-    def a2a_arrival(m, k):
-        slot = blend.at[m, band(k)]
-        return send(slot, slot, a2a_send.at[m, k - 1], a2a_recv.at[m, k - 1], (s, w, band(k)))
+    pairs = range(wqkv.shape[2] // 128)
+
+    def a2a_copy(m, k, pair):
+        columns = pl.ds(128 * pair, 128)
+        return send(bstage.at[m, band(k), :, columns], blend.at[m, b, :, columns],
+                    a2a_send.at[m, k - 1, pair], a2a_recv.at[m, bands - k - 1, pair], (s, w, band(k)))
+
+    def a2a_arrival(m, k, pair):
+        slot = blend.at[m, band(k), :, pl.ds(128 * pair, 128)]
+        return send(slot, slot, a2a_send.at[m, k - 1, pair], a2a_recv.at[m, k - 1, pair],
+                    (s, w, band(k)))
 
     def w_piece(slot, owner, chunk):
         start = (lax.rem(owner, 4) * 2 + chunk) * piece
@@ -271,12 +275,11 @@
             ).astype(jnp.bfloat16)
 
     def attend(m):
-        inner = projected.shape[2]
         rows = projected.shape[1]
         lane = lax.broadcasted_iota(jnp.int32, (rows, 128), 1)
-        for pair in range(inner // 128):
+        for pair in pairs:
             columns = slice(128 * pair, 128 * pair + 128)
-            queries = projected[0, :, columns]
+            queries = projected[0, :, columns] * (1.0 / math.sqrt(HEAD_DIM))
             keys_all = projected[1, :, columns]
             values_all = projected[2, :, columns]
             results = []
@@ -285,7 +288,7 @@
                 query = jnp.where(mine, queries, jnp.zeros_like(queries))
                 scores = lax.dot_general(
                     query, keys_all, (((1,), (1,)), ((), ())), preferred_element_type=jnp.float32
-                ) * (1.0 / math.sqrt(HEAD_DIM)) + bias[...]
+                ) + bias[...]
                 largest = jnp.max(scores, axis=-1, keepdims=True)
                 weights = jnp.exp(scores - largest)
                 total = jnp.sum(weights, axis=-1, keepdims=True)
@@ -299,13 +302,14 @@
             mixed = mixed.astype(jnp.bfloat16)
             for place in range(bands):
                 bstage[m, place, :, columns] = mixed[place * quad:(place + 1) * quad]
-        for k in others:
-            a2a_copy(m, k).start()
-        blend[m, b] = bstage[m, b]
+            for k in others:
+                a2a_copy(m, k, pair).start()
+            blend[m, b, :, columns] = bstage[m, b, :, columns]
 
     def finish(m):
         for k in others:
-            a2a_arrival(m, k).wait_recv()
+            for pair in pairs:
+                a2a_arrival(m, k, pair).wait_recv()
         for start in range(0, width, 512):
             columns = slice(start, start + 512)
             total = full[m, b, :, columns].astype(jnp.float32)
@@ -426,7 +430,8 @@
 
     for m in range(micros):
         for k in others:
-            a2a_copy(m, k).wait_send()
+            for pair in pairs:
+                a2a_copy(m, k, pair).wait_send()
     for chain in weight_chains:
         chain.drain()
     for k in others:
@@ -503,7 +508,7 @@
             pltpu.VMEM((micros, quad, width), bf16),
             pltpu.VMEM((micros, quad, width), bf16),
             dma((micros, 3)), dma((micros, 3, 2)),
-            dma((micros, 3)), dma((micros, 3)),
+            dma((micros, 3, inner // 128)), dma((micros, 3, inner // 128)),
             dma((micros, 2)), dma((micros, 2)),
             dma((micros, sections, 2)), dma((micros, 2)),
             dma((5, 2, 3)), dma((5, 2, 3)), dma((3, 3)),

time: 79.5 us -> 81.6 us (1.026)
  Pallas kernels: 77.8 us -> 79.8 us
    pallas_call x1, Pallas kernels: 77.8 us -> 79.8 us  [body(): pl.pallas_call(functools.partial(kernel, sections, windows, bands), out_s...]
where the time goes in v10:
time: 81.6 us; the launch traced here: 81.4 us
  Pallas kernels  79.8 us (98%)
  local copies, waits for them, and re-layouts  1.6 us (2%)
    pallas_call x1, Pallas kernels, body(): pl.pallas_call(functools.partial(kernel, sections, windows, bands), out_s...  79.8 us

profile of v10, /device:TPU:0, one launch (start us, length us, event | category | flops | bytes accessed | tf_op | source)
XLA Modules:
  0.0 81.4 jit_solution(3103571919260409777)
XLA Ops:
  0.0 79.8 %relay.1 = bf16[2,64,552]{2,1,0:T(8,128)(2,1)} custom-call(bf16[2,64,1536]{2,1,0:T(8,128)(2,1)} %bitcast.14, s32[1,256]{1,0:T(1,128)} %bitcast.15, f32[1,1536]{1,0:T(1,128)} %gain.1, bf16[3,1536,256]{2,1,0:T(8,128)(2,1)} %bitcast.10, bf16[256,1536]{1,0:T(8,128)(2,1)} %bitcast.12, f32[1536]{0:T(1024)} %final_gain.1, bf16[552,1536]{1,0:T(8,128)(2,1)} %bitcast.11), custom_call_target="tpu_custom_call" | custom-call | tf_op jit(solution)/shard_map/relay/pallas_call | solution.py:489
  79.8 1.6 %copy.10 = bf16[2,1,1,64,552]{4,3,2,1,0:T(8,128)(2,1)} copy(bf16[2,1,1,64,552]{4,3,2,1,0:T(8,128)(2,1)} %bitcast.13) | data formatting | bytes 282624
